TPU v7x, 32 devices: a whole 2x2x4 slice. The times are simulated.
32 devices in a mesh: replica: 4 (over y, x), fsdp: 8 (over z, core).
Axes of the slice: x: 2, y: 2, z: 4, core: 2. Of those that a mesh axis runs over, the one named last changes fastest.
Arguments:
- inputs: bfloat16 [8192, 4096], P(('replica', 'fsdp')), may hold values from -100 to 100
- out_grad: bfloat16 [8192, 512], P(('replica', 'fsdp')), may hold values from -1 to 1
- inner_weight: float32 [4, 4096, 512], P('replica', 'fsdp'), may hold values from -0.6 to 0.6
- adam_first: float32 [4, 4096, 512], P('replica', 'fsdp'), may hold values from -1.8 to 1.8
- adam_second: float32 [4, 4096, 512], P('replica', 'fsdp'), may hold values from 0.05 to 1
- fragment_local: float32 [4, 2, 8192, 1024], P('replica', None, 'fsdp'), may hold values from -3 to 3
- anchor: float32 [2, 8192, 1024], P(None, 'fsdp'), may hold values from -3 to 3
- outer_momentum: float32 [2, 8192, 1024], P(None, 'fsdp'), may hold values from -1.8 to 1.8
- outer_prev: float32 [2, 8192, 1024], P(None, 'fsdp'), may hold values from -1.8 to 1.8
Outputs:
- new_weight: float32 [4, 4096, 512], P('replica', 'fsdp')
- new_first: float32 [4, 4096, 512], P('replica', 'fsdp')
- new_second: float32 [4, 4096, 512], P('replica', 'fsdp')
- outer_delta: float32 [2, 8192, 1024], P(None, 'fsdp')
- new_momentum: float32 [2, 8192, 1024], P(None, 'fsdp')
- new_anchor: float32 [2, 8192, 1024], P(None, 'fsdp')
All inputs are finite; a program needn't handle non-finite values.
Results may differ from a plain program's by a relative error of at most 0.0003.
Values may be sent and summed in bfloat16 or wider, within the bound.
A program may use at most 192 MiB of HBM per device.

v0:
```python
import math

import jax
import jax.numpy as jnp
from jax import lax
from jax.sharding import PartitionSpec as P

first_decay = 0.9
second_decay = 0.95
inner_rate = 0.02
outer_rate = 0.7
outer_mu = 0.9
clip_rms = 4.0
adam_eps = 1e-08
norm_eps = 1e-06


def outer_mean(anchor, fragment_local):
    spread = anchor - fragment_local[0]
    return lax.psum(spread, "replica") / lax.axis_size("replica")


def body(
    inputs,
    out_grad,
    inner_weight,
    adam_first,
    adam_second,
    fragment_local,
    anchor,
    outer_momentum,
    outer_prev,
):
    groups = lax.axis_size("fsdp")
    feature_rows = inner_weight.shape[1]
    out_features = inner_weight.shape[2]
    grad_shard = lax.psum_scatter(
        lax.dot_general(
            inputs, out_grad, (((0,), (0,)), ((), ())), preferred_element_type=jnp.float32
        ),
        "fsdp",
        scatter_dimension=0,
        tiled=True,
    )
    norm_sq = lax.psum(jnp.sum(grad_shard * grad_shard), "fsdp")
    clip_limit = clip_rms * math.sqrt(feature_rows * groups * out_features)
    factor = jnp.minimum(1.0, clip_limit / jnp.sqrt(norm_sq + norm_eps))
    clipped = (grad_shard * factor)[None]
    new_first = first_decay * adam_first + (1.0 - first_decay) * clipped
    new_second = second_decay * adam_second + (1.0 - second_decay) * clipped * clipped
    new_weight = inner_weight - inner_rate * new_first / (jnp.sqrt(new_second) + adam_eps)
    new_momentum = outer_mu * outer_momentum + outer_prev
    new_anchor = anchor - outer_rate * (outer_prev + outer_mu * new_momentum)
    outer_delta = outer_mean(anchor, fragment_local)
    return (new_weight, new_first, new_second, outer_delta, new_momentum, new_anchor)


def solution(mesh):
    placed = (
        P(("replica", "fsdp"), None),
        P(("replica", "fsdp"), None),
        P("replica", "fsdp", None),
        P("replica", "fsdp", None),
        P("replica", "fsdp", None),
        P("replica", None, "fsdp", None),
        P(None, "fsdp", None),
        P(None, "fsdp", None),
        P(None, "fsdp", None),
    )
    return jax.shard_map(
        body,
        mesh=mesh,
        in_specs=placed,
        out_specs=(
            P("replica", "fsdp", None),
            P("replica", "fsdp", None),
            P("replica", "fsdp", None),
            P(None, "fsdp", None),
            P(None, "fsdp", None),
            P(None, "fsdp", None),
        ),
        check_vma=False,
    )
```

profile of v0, /device:TPU:0, one launch (start us, length us, event | category | flops | bytes accessed | tf_op | source)
XLA Modules:
  0.0 250.4 jit_solution(3947400816324739359)
XLA Ops:
  8.0 0.0 copy-start
  8.0 0.0 reduce-scatter.2.cloned.1.call-start
  8.1 1.5 copy-done
  9.6 5.6 %fusion.3 = f32[4096,512]{1,0:T(8,128)} fusion(bf16[256,4096]{1,0:T(8,128)(2,1)S(1)} %copy-done, bf16[256,512]{1,0:T(8,128)(2,1)} %param.10), kind=kOutput, calls=%fused_computation.10 | convolution fusion | flops 1073741824 | bytes 10747904 | tf_op jit(solution)/shard_map/dot_general | solution.py:38
  15.2 0.0 reduce-scatter.2.cloned.1.call-update
  15.3 0.0 all-reduce.2.cloned.1.call-start
  15.3 21.9 %multiply_subtract_fusion = (f32[2,1024,1024]{2,1,0:T(8,128)}, f32[2,1024,1024]{2,1,0:T(8,128)}, f32[2,1024,1024]{2,1,0:T(8,128)}) fusion(f32[2,1024,1024]{2,1,0:T(8,128)} %param.15, f32[2,1024,1024]{2,1,0:T(8,128)} %param.17, f32[2,1024,1024]{2,1,0:T(8,128)} %param.16, f32[1,2,1024,1024]{3,2,1,0:T(8,128)} %param.14), kind=kLoop, calls=%fused_computation.1 | loop fusion | flops 14680064 | bytes 58720256 | tf_op jit(solution)/shard_map/sub | solution.py:53
  37.2 0.0 all-reduce.2.cloned.1.call-update
  37.2 70.5 %reduce-scatter.2.cloned.1.call-done = f32[512,512]{1,0:T(8,128)} async-done(((f32[4096,512]{1,0:T(8,128)}), f32[512,512]{1,0:T(8,128)}) %reduce-scatter.2.cloned.1.call-update) | async-done | bytes 1048592 | tf_op jit(solution)/shard_map/reduce_scatter | solution.py:37
  107.7 0.0 copy-start.1
  107.7 2.2 multiply_reduce_fusion
  110.0 0.0 copy-start.2
  110.0 102.7 %all-reduce.2.cloned.1.call-done = f32[2,1024,1024]{2,1,0:T(8,128)} async-done(((f32[2,1024,1024]{2,1,0:T(8,128)}), f32[2,1024,1024]{2,1,0:T(8,128)}) %all-reduce.2.cloned.1.call-update) | async-done | bytes 8388624 | tf_op jit(solution)/shard_map/psum | solution.py:20
  212.7 8.7 %broadcast_multiply_fusion = f32[2,1024,1024]{2,1,0:T(8,128)} fusion(f32[2,1024,1024]{2,1,0:T(8,128)} %all-reduce.2.cloned.1.call-done), kind=kLoop, calls=%fused_computation.3 | loop fusion | flops 2097152 | bytes 16777216 | tf_op jit(solution)/shard_map/div | solution.py:20
  221.4 16.9 %psum.14 = f32[]{:T(128)} all-reduce(f32[]{:T(128)} %multiply_reduce_fusion), channel_id=1, replica_groups=mesh['replica'=4,'fsdp'=8] {'fsdp'}, use_global_device_ids=true, to_apply=%region_2.0 | all-reduce | flops 1 | bytes 8 | tf_op jit(solution)/shard_map/psum | solution.py:45
  238.9 0.0 copy-done.2
  239.0 4.0 %divide_subtract_fusion = (f32[1,512,512]{2,1,0:T(8,128)}, f32[1,512,512]{2,1,0:T(8,128)}, f32[1,512,512]{2,1,0:T(8,128)}) fusion(f32[1,512,512]{2,1,0:T(8,128)} %param.11, f32[512,512]{1,0:T(8,128)S(1)} %copy-done.2, f32[]{:T(128)S(6)} %min_shard_map.3, f32[1,512,512]{2,1,0:T(8,128)} %param.12, f32[1,512,512]{2,1,0:T(8,128)} %param.13), kind=kLoop, calls=%fused_computation.8 | loop fusion | flops 3145728 | bytes 7340036 | tf_op jit(solution)/shard_map/sub | solution.py:51
  242.9 0.0 copy-done.1
Async XLA Ops:
  8.0 1.6 copy-start
  8.0 99.7 %reduce-scatter.2.cloned.1.call-start = ((), (), s32[]{:S(2)}) async-start(), calls=%async_computation.1 | async-start | bytes 9437184 | tf_op jit(solution)/shard_map/reduce_scatter | solution.py:37
  15.3 197.4 %all-reduce.2.cloned.1.call-start = ((), (), s32[]{:S(2)}) async-start(), calls=%async_computation.2 | async-start | bytes 16777216 | tf_op jit(solution)/shard_map/psum | solution.py:20
  107.7 135.2 %copy-start.1 = (bf16[256,4096]{1,0:T(8,128)(2,1)S(1)}, bf16[256,4096]{1,0:T(8,128)(2,1)}, u32[]{:S(2)}) copy-start(bf16[256,4096]{1,0:T(8,128)(2,1)} %param.9) | copy-start | bytes 6291460
  110.0 129.0 %copy-start.2 = (f32[512,512]{1,0:T(8,128)S(1)}, f32[512,512]{1,0:T(8,128)}, u32[]{:S(2)}) copy-start(f32[512,512]{1,0:T(8,128)} %reduce-scatter.2.cloned.1.call-done) | copy-start | bytes 3145732
Sparse Core Ops, SparseCore 0:
  15.4 92.3 reduce-scatter.1
Sparse Core Ops, SparseCore 1:
  37.3 175.3 all-reduce.1
where the time goes:
time: 251 us; the launch traced here: 250 us
  waiting for transfers between devices  173 us (69%)
  other arithmetic  36.8 us (15%)
  blocking collectives  16.9 us (7%)
  between operations  16.2 us (6%)
  matrix products  5.64 us (2%)
    psum x1, waiting for transfers between devices, outer_mean(): return lax.psum(spread, 'replica') / lax.axis_size('replica')  103 us
    reduce_scatter x1, waiting for transfers between devices, body(): lax.psum_scatter(lax.dot_general(inputs, out_grad, (((0,), (0,)), ((), ()...  70.5 us
    sub x1, other arithmetic, body(): new_anchor = anchor - outer_rate * (outer_prev + outer_mu * new_momentum)  21.9 us
    psum x1, blocking collectives, body(): norm_sq = lax.psum(jnp.sum(grad_shard * grad_shard), 'fsdp')  16.9 us
    div x1, other arithmetic, outer_mean(): return lax.psum(spread, 'replica') / lax.axis_size('replica')  8.7 us
    dot_general x1, matrix products, body(): lax.dot_general(inputs, out_grad, (((0,), (0,)), ((), ())), preferred_ele...  5.64 us
  transfers between devices with their start and end apart: 2, of which 2 were waited for; matrix products, arithmetic and copies ran while one was open for 10% of the time, Pallas kernels for 0%

commit v1 on v0

--- a/solution.py
+++ b/solution.py
@@ -1,8 +1,11 @@
+import functools
 import math
 
 import jax
 import jax.numpy as jnp
 from jax import lax
+from jax.experimental import pallas as pl
+from jax.experimental.pallas import tpu as pltpu
 from jax.sharding import PartitionSpec as P
 
 first_decay = 0.9
@@ -15,9 +18,204 @@
 norm_eps = 1e-06
 
 
+KIND_A, KIND_B, KIND_C, KIND_G0, KIND_G1, KIND_F = range(6)
+SPAN = 172.0
+HALF_SPAN = 86.0
+PIECES = 2
+STEP_ROWS = 32
+
+
+def outer_kernel(rows, width, local_ref, anchor_ref, out_ref, vf, va, sent, held, load_sem, store_sem, send_sem, recv_sem):
+    me = lax.axis_index("replica")
+    ny = (me + 2) % 4
+    nx = 3 - ny
+    diag = 3 - me
+    neighbour = (nx, ny)
+    owners = (diag, nx, ny, me)
+    steps = rows // STEP_ROWS
+
+    loads = []
+    for j in range(4):
+        part = pl.ds(pl.multiple_of(owners[j] * rows, rows), rows)
+        loads.append(
+            (
+                pltpu.make_async_copy(local_ref.at[part, :], vf.at[j], load_sem.at[j, 0]),
+                pltpu.make_async_copy(anchor_ref.at[part, :], va.at[j], load_sem.at[j, 1]),
+            )
+        )
+    for pair in loads:
+        for load in pair:
+            load.start()
+
+    barrier = pltpu.get_barrier_semaphore()
+    for n in neighbour:
+        pl.semaphore_signal(barrier, inc=1, device_id={"replica": n}, device_id_type=pl.DeviceIdType.MESH)
+    pl.semaphore_wait(barrier, 2)
+
+    def columns(half, k):
+        return pl.ds((half * PIECES + k) * width, width)
+
+    def copy(kind, way, k):
+        if kind == KIND_F:
+            src = held.at[KIND_G1 if way == 0 else KIND_G0, 1 - way, k]
+        elif kind in (KIND_G0, KIND_G1):
+            src = sent.at[kind, 0, k]
+        else:
+            src = sent.at[kind, way, k]
+        return pltpu.make_async_remote_copy(
+            src_ref=src,
+            dst_ref=held.at[kind, way, k],
+            send_sem=send_sem.at[kind, way, k],
+            recv_sem=recv_sem.at[kind, way, k],
+            device_id={"replica": neighbour[way]},
+            device_id_type=pl.DeviceIdType.MESH,
+        )
+
+    def scale_of(box, kind, way, k):
+        return box[kind, way, k, rows : rows + 16, :].astype(jnp.float32)[0:1] * (1.0 / SPAN)
+
+    def decoded(box, kind, way, k, scale, r):
+        code = box[kind, way, k, r, :].astype(jnp.float32)
+        size = (jnp.log(jnp.abs(code)) + HALF_SPAN) * scale
+        return jnp.where(code < 0.0, -size, size)
+
+    def encode(j, half, k, kind, way, terms, factor=None):
+        cs = columns(half, k)
+        scales = [scale_of(held, t[0], t[1], k) for t in terms]
+
+        def gather(i, top):
+            r = pl.ds(pl.multiple_of(i * STEP_ROWS, STEP_ROWS), STEP_ROWS)
+            x = va[j, r, cs] - vf[j, r, cs]
+            for t, s in zip(terms, scales):
+                x = x + decoded(held, t[0], t[1], k, s, r)
+            if factor is not None:
+                x = x * factor
+            vf[j, r, cs] = x
+            return jnp.maximum(top, jnp.max(jnp.abs(x).reshape(STEP_ROWS // 8, 8, width), axis=0))
+
+        top = lax.fori_loop(0, steps, gather, jnp.zeros((8, width), jnp.float32))
+        top = (jnp.max(top, axis=0, keepdims=True) * 1.01 + 1e-30).astype(jnp.bfloat16)
+        sent[kind, way, k, rows : rows + 16, :] = jnp.broadcast_to(top.astype(jnp.float32), (16, width)).astype(
+            jnp.bfloat16
+        )
+        slope = SPAN / top.astype(jnp.float32)
+
+        def write(i, c):
+            r = pl.ds(pl.multiple_of(i * STEP_ROWS, STEP_ROWS), STEP_ROWS)
+            x = vf[j, r, cs]
+            y = jnp.exp(jnp.abs(x) * slope - HALF_SPAN)
+            sent[kind, way, k, r, :] = jnp.where(x < 0.0, -y, y).astype(jnp.bfloat16)
+            return c
+
+        lax.fori_loop(0, steps, write, 0)
+
+    def unfold(j, half, k, box, kind, way):
+        cs = columns(half, k)
+        scale = scale_of(box, kind, way, k)
+
+        def step(i, c):
+            r = pl.ds(pl.multiple_of(i * STEP_ROWS, STEP_ROWS), STEP_ROWS)
+            vf[j, r, cs] = decoded(box, kind, way, k, scale, r)
+            return c
+
+        lax.fori_loop(0, steps, step, 0)
+
+    def loaded(j):
+        for load in loads[j]:
+            load.wait()
+
+    loaded(0)
+    for k in range(PIECES):
+        for way in (0, 1):
+            encode(0, 1 - way, k, KIND_A, way, ())
+            copy(KIND_A, way, k).start()
+    loaded(1)
+    loaded(2)
+    for k in range(PIECES):
+        for way in (0, 1):
+            encode(1 + way, 1 - way, k, KIND_B, way, ())
+            copy(KIND_B, way, k).start()
+    for k in range(PIECES):
+        for way in (0, 1):
+            copy(KIND_A, 1 - way, k).wait_recv()
+            encode(1 + way, way, k, KIND_C, way, ((KIND_A, 1 - way),))
+            copy(KIND_C, way, k).start()
+    loaded(3)
+    for k in range(PIECES):
+        for half in (0, 1):
+            copy(KIND_B, 1 - half, k).wait_recv()
+            copy(KIND_C, half, k).wait_recv()
+            encode(3, half, k, KIND_G0 + half, 0, ((KIND_B, 1 - half), (KIND_C, half)), 0.25)
+            for way in (0, 1):
+                copy(KIND_G0 + half, way, k).start()
+
+    def store(j):
+        part = pl.ds(pl.multiple_of(owners[j] * rows, rows), rows)
+        return pltpu.make_async_copy(vf.at[j], out_ref.at[part, :], store_sem.at[j])
+
+    for k in range(PIECES):
+        for half in (0, 1):
+            unfold(3, half, k, sent, KIND_G0 + half, 0)
+    store(3).start()
+    for k in range(PIECES):
+        for way in (0, 1):
+            first = KIND_G1 if way == 0 else KIND_G0
+            copy(first, 1 - way, k).wait_recv()
+            copy(KIND_F, way, k).start()
+    for k in range(PIECES):
+        for way in (0, 1):
+            unfold(1 + way, way, k, held, KIND_G0 + way, way)
+    for way in (0, 1):
+        for k in range(PIECES):
+            late = 1 - way
+            copy(KIND_G0 + late, way, k).wait_recv()
+            unfold(1 + way, late, k, held, KIND_G0 + late, way)
+        store(1 + way).start()
+    for k in range(PIECES):
+        for way in (0, 1):
+            copy(KIND_F, way, k).wait_recv()
+            unfold(0, 1 - way, k, held, KIND_F, way)
+    store(0).start()
+    for kind in range(6):
+        for way in (0, 1):
+            for k in range(PIECES):
+                copy(kind, way, k).wait_send()
+    for j in range(4):
+        store(j).wait()
+
+
 def outer_mean(anchor, fragment_local):
-    spread = anchor - fragment_local[0]
-    return lax.psum(spread, "replica") / lax.axis_size("replica")
+    replicas = lax.axis_size("replica")
+    layers, depth, width = anchor.shape
+    rows = layers * depth // 4
+    piece = width // (2 * PIECES)
+    if replicas != 4 or (layers * depth) % (4 * STEP_ROWS) != 0 or width % (256 * PIECES) != 0:
+        spread = anchor - fragment_local[0]
+        return lax.psum(spread, "replica") / replicas
+    sems = pltpu.SemaphoreType.DMA
+    mean = pl.pallas_call(
+        functools.partial(outer_kernel, rows, piece),
+        out_shape=jax.ShapeDtypeStruct((4 * rows, width), jnp.float32),
+        in_specs=[pl.BlockSpec(memory_space=pl.ANY)] * 2,
+        out_specs=pl.BlockSpec(memory_space=pl.ANY),
+        scratch_shapes=[
+            pltpu.VMEM((4, rows, width), jnp.float32),
+            pltpu.VMEM((4, rows, width), jnp.float32),
+            pltpu.VMEM((5, 2, PIECES, rows + 16, piece), jnp.bfloat16),
+            pltpu.VMEM((6, 2, PIECES, rows + 16, piece), jnp.bfloat16),
+            sems((4, 2)),
+            sems((4,)),
+            sems((6, 2, PIECES)),
+            sems((6, 2, PIECES)),
+        ],
+        compiler_params=pltpu.CompilerParams(
+            collective_id=0, has_side_effects=True, vmem_limit_bytes=48 * 1024 * 1024
+        ),
+        cost_estimate=pl.CostEstimate(
+            flops=40 * layers * depth * width, bytes_accessed=12 * layers * depth * width, transcendentals=0
+        ),
+    )(fragment_local.reshape(4 * rows, width), anchor.reshape(4 * rows, width))
+    return mean.reshape(anchor.shape)
 
 
 def body(

time: 251 us -> 146 us (0.58)
  waiting for transfers between devices: 173 us -> 0.02 us
  Pallas kernels: 0 us -> 78.5 us
  other arithmetic: 36.8 us -> 20.1 us
  local copies, waits for them, and re-layouts: 1.55 us -> 10.2 us
    psum x1 -> x0, waiting for transfers between devices: 103 us -> none  [outer_mean(): return lax.psum(spread, 'replica') / lax.axis_size('replica')]
    pallas_call x0 -> x1, Pallas kernels: none -> 78.5 us  [outer_mean(): pl.pallas_call(functools.partial(outer_kernel, rows, piece), out_shape=ja...]
    reduce_scatter x1, waiting for transfers between devices: 70.5 us -> 0.01 us  [body(): lax.psum_scatter(lax.dot_general(inputs, out_grad, (((0,), (0,)), ((), ()...]
    div x1 -> x0, other arithmetic: 8.7 us -> none  [outer_mean(): return lax.psum(spread, 'replica') / lax.axis_size('replica')]
    unnamed x6 -> x11, local copies, waits for them, and re-layouts: 1.55 us -> 10.2 us
    sub x1, other arithmetic: 21.9 us -> 14.7 us  [body(): new_anchor = anchor - outer_rate * (outer_prev + outer_mu * new_momentum)]
  transfers between devices with their start and end apart: 2 -> 1, of which waited for: 2 -> 0; matrix products, arithmetic and copies ran while one was open for 10% -> 10% of each run, Pallas kernels for 0% -> 54%
where the time goes in v1:
time: 146 us
  Pallas kernels  78.5 us (54%)
  other arithmetic  20.1 us (14%)
  blocking collectives  16.8 us (12%)
  between operations  14.8 us (10%)
  local copies, waits for them, and re-layouts  10.2 us (7%)
  matrix products  5.64 us (4%)
    pallas_call x1, Pallas kernels, outer_mean(): pl.pallas_call(functools.partial(outer_kernel, rows, piece), out_shape=ja...  78.5 us
    psum x1, blocking collectives, body(): norm_sq = lax.psum(jnp.sum(grad_shard * grad_shard), 'fsdp')  16.8 us
    sub x1, other arithmetic, body(): new_anchor = anchor - outer_rate * (outer_prev + outer_mu * new_momentum)  14.7 us
    unnamed x11, local copies, waits for them, and re-layouts  10.2 us
    dot_general x1, matrix products, body(): lax.dot_general(inputs, out_grad, (((0,), (0,)), ((), ())), preferred_ele...  5.64 us
    sub x1, other arithmetic, body(): inner_weight - inner_rate * new_first / (jnp.sqrt(new_second) + adam_eps)  3.32 us
  transfers between devices with their start and end apart: 1, of which 0 were waited for; matrix products, arithmetic and copies ran while one was open for 10% of the time, Pallas kernels for 54%

profile of v1, /device:TPU:0, one launch (start us, length us, event | category | flops | bytes accessed | tf_op | source)
XLA Modules:
  0.0 146.2 jit_solution(9416971099219027693)
XLA Ops:
  7.2 0.0 copy-start
  7.2 0.0 reduce-scatter.2.cloned.1.call-start
  7.2 1.5 %copy-done = bf16[256,4096]{1,0:T(8,128)(2,1)S(1)} copy-done((bf16[256,4096]{1,0:T(8,128)(2,1)S(1)}, bf16[256,4096]{1,0:T(8,128)(2,1)}, u32[]{:S(2)}) %copy-start) | copy-done | bytes 2097176
  8.8 5.6 %fusion.3 = f32[4096,512]{1,0:T(8,128)} fusion(bf16[256,4096]{1,0:T(8,128)(2,1)S(1)} %copy-done, bf16[256,512]{1,0:T(8,128)(2,1)} %param.10), kind=kOutput, calls=%fused_computation.8 | convolution fusion | flops 1073741824 | bytes 10747904 | tf_op jit(solution)/shard_map/dot_general | solution.py:236
  14.4 0.0 reduce-scatter.2.cloned.1.call-update
  14.4 78.5 %shard_map.136 = f32[2048,1024]{1,0:T(8,128)} custom-call(f32[2048,1024]{1,0:T(8,128)} %bitcast.15, f32[2048,1024]{1,0:T(8,128)} %bitcast.13), custom_call_target="tpu_custom_call" | custom-call | flops 83886080 | bytes 25165824 | tf_op jit(solution)/shard_map/pallas_call | solution.py:196
  93.0 0.0 copy-start.2
  93.0 0.0 copy-start.3
  93.0 0.0 copy-start.4
  93.0 14.7 %multiply_subtract_fusion = (f32[2,1024,1024]{2,1,0:T(8,128)}, f32[2,1024,1024]{2,1,0:T(8,128)}) fusion(f32[2,1024,1024]{2,1,0:T(8,128)} %param.15, f32[2,1024,1024]{2,1,0:T(8,128)} %param.17, f32[2,1024,1024]{2,1,0:T(8,128)} %param.16), kind=kLoop, calls=%fused_computation | loop fusion | flops 12582912 | bytes 41943040 | tf_op jit(solution)/shard_map/sub | solution.py:251
  107.7 0.0 reduce-scatter.2.cloned.1.call-done
  107.7 2.1 %multiply_reduce_fusion = f32[]{:T(128)} fusion(f32[512,512]{1,0:T(8,128)} %reduce-scatter.2.cloned.1.call-done), kind=kLoop, calls=%fused_computation.7 | loop fusion | flops 524287 | bytes 1048580 | tf_op jit(solution)/shard_map/reduce_sum | solution.py:243
  109.8 16.8 %psum.7 = f32[]{:T(128)} all-reduce(f32[]{:T(128)} %multiply_reduce_fusion), channel_id=1, replica_groups=mesh['replica'=4,'fsdp'=8] {'fsdp'}, use_global_device_ids=true, to_apply=%region_2.0 | all-reduce | flops 1 | bytes 8 | tf_op jit(solution)/shard_map/psum | solution.py:243
  127.4 0.0 copy-done.2
  127.4 0.0 copy-done.3
  127.4 0.0 copy-done.4
  127.4 3.3 %divide_subtract_fusion = (f32[1,512,512]{2,1,0:T(8,128)}, f32[1,512,512]{2,1,0:T(8,128)}, f32[1,512,512]{2,1,0:T(8,128)}) fusion(f32[1,512,512]{2,1,0:T(8,128)S(1)} %copy-done.2, f32[512,512]{1,0:T(8,128)} %reduce-scatter.2.cloned.1.call-done, f32[]{:T(128)S(6)} %min_shard_map.3, f32[1,512,512]{2,1,0:T(8,128)S(1)} %copy-done.3, f32[1,512,512]{2,1,0:T(8,128)S(1)} %copy-done.4), kind=kLoop, calls=%fused_computation.6 | loop fusion | flops 3145728 | bytes 7340036 | tf_op jit(solution)/shard_map/sub | solution.py:249
  130.7 0.0 copy-start.1
  130.7 8.6 %copy.16 = f32[2,1024,1024]{2,1,0:T(8,128)} copy(f32[2,1024,1024]{2,1,0:T(8,128)} %bitcast.14) | data formatting | bytes 16777216
  139.3 0.0 copy-done.1
Async XLA Ops:
  7.2 1.6 %copy-start = (bf16[256,4096]{1,0:T(8,128)(2,1)S(1)}, bf16[256,4096]{1,0:T(8,128)(2,1)}, u32[]{:S(2)}) copy-start(bf16[256,4096]{1,0:T(8,128)(2,1)} %param.9) | copy-start | bytes 6291460
  7.2 100.5 %reduce-scatter.2.cloned.1.call-start = ((), (), s32[]{:S(2)}) async-start(), calls=%async_computation.1 | async-start | bytes 9437184 | tf_op jit(solution)/shard_map/reduce_scatter | solution.py:235
  93.0 34.4 %copy-start.2 = (f32[1,512,512]{2,1,0:T(8,128)S(1)}, f32[1,512,512]{2,1,0:T(8,128)}, u32[]{:S(2)}) copy-start(f32[1,512,512]{2,1,0:T(8,128)} %param.11) | copy-start | bytes 3145732
  93.0 34.4 %copy-start.3 = (f32[1,512,512]{2,1,0:T(8,128)S(1)}, f32[1,512,512]{2,1,0:T(8,128)}, u32[]{:S(2)}) copy-start(f32[1,512,512]{2,1,0:T(8,128)} %param.12) | copy-start | bytes 3145732
  93.0 34.4 %copy-start.4 = (f32[1,512,512]{2,1,0:T(8,128)S(1)}, f32[1,512,512]{2,1,0:T(8,128)}, u32[]{:S(2)}) copy-start(f32[1,512,512]{2,1,0:T(8,128)} %param.13) | copy-start | bytes 3145732
  130.7 8.6 %copy-start.1 = (bf16[256,4096]{1,0:T(8,128)(2,1)S(1)}, bf16[256,4096]{1,0:T(8,128)(2,1)}, u32[]{:S(2)}) copy-start(bf16[256,4096]{1,0:T(8,128)(2,1)} %param.9) | copy-start | bytes 6291460
Sparse Core Ops, SparseCore 0:
  14.5 92.3 reduce-scatter.1

commit v2 on v1

--- a/solution.py
+++ b/solution.py
@@ -25,7 +25,35 @@
 STEP_ROWS = 32
 
 
-def outer_kernel(rows, width, local_ref, anchor_ref, out_ref, vf, va, sent, held, load_sem, store_sem, send_sem, recv_sem):
+def outer_kernel(
+    rows,
+    width,
+    group,
+    local_ref,
+    anchor_ref,
+    grad_ref,
+    out_ref,
+    shard_ref,
+    norm_ref,
+    vf,
+    va,
+    sent,
+    held,
+    load_sem,
+    store_sem,
+    send_sem,
+    recv_sem,
+    own,
+    twin,
+    grad_sent,
+    grad_held,
+    part_sent,
+    part_held,
+    own_sem,
+    twin_sem,
+    grad_sem,
+    part_sem,
+):
     me = lax.axis_index("replica")
     ny = (me + 2) % 4
     nx = 3 - ny
@@ -33,6 +61,48 @@
     neighbour = (nx, ny)
     owners = (diag, nx, ny, me)
     steps = rows // STEP_ROWS
+
+    place = lax.axis_index("fsdp")
+    core = place % 2
+    chip = place // 2
+    chips = group // 2
+    block = shard_ref.shape[0]
+    grad_steps = block // STEP_ROWS
+
+    def own_copy(s):
+        start = pl.multiple_of((((chip + s) % chips) * 2 + core) * block, block)
+        return pltpu.make_async_copy(grad_ref.at[pl.ds(start, block), :], own.at[s], own_sem.at[s])
+
+    def twin_copy(s):
+        start = pl.multiple_of((((chip + s) % chips) * 2 + 1 - core) * block, block)
+        return pltpu.make_async_remote_copy(
+            src_ref=grad_ref.at[pl.ds(start, block), :],
+            dst_ref=twin.at[s],
+            send_sem=twin_sem.at[0, s],
+            recv_sem=twin_sem.at[1, s],
+            device_id={"fsdp": chip * 2 + 1 - core},
+            device_id_type=pl.DeviceIdType.MESH,
+        )
+
+    def grad_copy(s):
+        return pltpu.make_async_remote_copy(
+            src_ref=grad_sent.at[s - 1],
+            dst_ref=grad_held.at[s - 1],
+            send_sem=grad_sem.at[0, s - 1],
+            recv_sem=grad_sem.at[1, s - 1],
+            device_id={"fsdp": ((chip + s) % chips) * 2 + core},
+            device_id_type=pl.DeviceIdType.MESH,
+        )
+
+    def part_copy(s):
+        return pltpu.make_async_remote_copy(
+            src_ref=part_sent,
+            dst_ref=part_held.at[s - 1],
+            send_sem=part_sem.at[0, s - 1],
+            recv_sem=part_sem.at[1, s - 1],
+            device_id={"fsdp": (place + s) % group},
+            device_id_type=pl.DeviceIdType.MESH,
+        )
 
     loads = []
     for j in range(4):
@@ -50,7 +120,15 @@
     barrier = pltpu.get_barrier_semaphore()
     for n in neighbour:
         pl.semaphore_signal(barrier, inc=1, device_id={"replica": n}, device_id_type=pl.DeviceIdType.MESH)
-    pl.semaphore_wait(barrier, 2)
+    for s in range(1, group):
+        pl.semaphore_signal(
+            barrier, inc=1, device_id={"fsdp": (place + s) % group}, device_id_type=pl.DeviceIdType.MESH
+        )
+    pl.semaphore_wait(barrier, group + 1)
+
+    for s in range(chips):
+        own_copy(s).start()
+        twin_copy(s).start()
 
     def columns(half, k):
         return pl.ds((half * PIECES + k) * width, width)
@@ -124,6 +202,52 @@
         for load in loads[j]:
             load.wait()
 
+    def encode_grad(s):
+        span = own.shape[2]
+
+        def gather(i, top):
+            r = pl.ds(pl.multiple_of(i * STEP_ROWS, STEP_ROWS), STEP_ROWS)
+            x = own[s, r, :] + twin[s, r, :]
+            own[s, r, :] = x
+            return jnp.maximum(top, jnp.max(jnp.abs(x).reshape(STEP_ROWS // 8, 8, span), axis=0))
+
+        top = lax.fori_loop(0, grad_steps, gather, jnp.zeros((8, span), jnp.float32))
+        top = (jnp.max(top, axis=0, keepdims=True) * 1.01 + 1e-30).astype(jnp.bfloat16).astype(jnp.float32)
+        grad_sent[s - 1, block : block + 16, :] = jnp.broadcast_to(top, (16, span)).astype(jnp.bfloat16)
+        slope = SPAN / top
+
+        def write(i, c):
+            r = pl.ds(pl.multiple_of(i * STEP_ROWS, STEP_ROWS), STEP_ROWS)
+            x = own[s, r, :]
+            y = jnp.exp(jnp.abs(x) * slope - HALF_SPAN)
+            grad_sent[s - 1, r, :] = jnp.where(x < 0.0, -y, y).astype(jnp.bfloat16)
+            return c
+
+        lax.fori_loop(0, grad_steps, write, 0)
+
+    def reduce_grad():
+        span = own.shape[2]
+        scales = [
+            grad_held[s - 1, block : block + 16, :].astype(jnp.float32)[0:1] * (1.0 / SPAN)
+            for s in range(1, chips)
+        ]
+
+        def step(i, squares):
+            r = pl.ds(pl.multiple_of(i * STEP_ROWS, STEP_ROWS), STEP_ROWS)
+            x = own[0, r, :] + twin[0, r, :]
+            for s in range(1, chips):
+                code = grad_held[s - 1, r, :].astype(jnp.float32)
+                size = (jnp.log(jnp.abs(code)) + HALF_SPAN) * scales[s - 1]
+                x = x + jnp.where(code < 0.0, -size, size)
+            own[0, r, :] = x
+            return squares + jnp.sum((x * x).reshape(STEP_ROWS // 8, 8, span), axis=0)
+
+        squares = lax.fori_loop(0, grad_steps, step, jnp.zeros((8, span), jnp.float32))
+        total = squares[:, 0:128]
+        for c in range(1, span // 128):
+            total = total + squares[:, c * 128 : (c + 1) * 128]
+        part_sent[...] = total
+
     loaded(0)
     for k in range(PIECES):
         for way in (0, 1):
@@ -135,6 +259,11 @@
         for way in (0, 1):
             encode(1 + way, 1 - way, k, KIND_B, way, ())
             copy(KIND_B, way, k).start()
+    for s in (2, 1, 3) if chips == 4 else range(1, chips):
+        own_copy(s).wait()
+        twin_copy(s).wait_recv()
+        encode_grad(s)
+        grad_copy(s).start()
     for k in range(PIECES):
         for way in (0, 1):
             copy(KIND_A, 1 - way, k).wait_recv()
@@ -148,6 +277,16 @@
             encode(3, half, k, KIND_G0 + half, 0, ((KIND_B, 1 - half), (KIND_C, half)), 0.25)
             for way in (0, 1):
                 copy(KIND_G0 + half, way, k).start()
+
+    own_copy(0).wait()
+    twin_copy(0).wait_recv()
+    for s in range(1, chips):
+        grad_copy(s).wait_recv()
+    reduce_grad()
+    for s in range(1, group):
+        part_copy(s).start()
+    shard_store = pltpu.make_async_copy(own.at[0], shard_ref, own_sem.at[0])
+    shard_store.start()
 
     def store(j):
         part = pl.ds(pl.multiple_of(owners[j] * rows, rows), rows)
@@ -176,6 +315,18 @@
             copy(KIND_F, way, k).wait_recv()
             unfold(0, 1 - way, k, held, KIND_F, way)
     store(0).start()
+    norm = part_sent[...]
+    for s in range(1, group):
+        part_copy(s).wait_recv()
+        norm = norm + part_held[s - 1]
+    norm_ref[...] = norm
+    shard_store.wait()
+    for s in range(chips):
+        twin_copy(s).wait_send()
+    for s in range(1, chips):
+        grad_copy(s).wait_send()
+    for s in range(1, group):
+        part_copy(s).wait_send()
     for kind in range(6):
         for way in (0, 1):
             for k in range(PIECES):
@@ -184,20 +335,40 @@
         store(j).wait()
 
 
-def outer_mean(anchor, fragment_local):
-    replicas = lax.axis_size("replica")
+def fits(anchor, grad, feature_rows):
     layers, depth, width = anchor.shape
+    return (
+        lax.axis_size("replica") == 4
+        and (layers * depth) % (4 * STEP_ROWS) == 0
+        and width % (256 * PIECES) == 0
+        and lax.axis_size("fsdp") == 8
+        and feature_rows % STEP_ROWS == 0
+        and grad.shape[1] % 128 == 0
+        and layers * depth * width <= 2 * 1024 * 1024
+    )
+
+
+def joint_sums(anchor, fragment_local, grad, feature_rows):
+    layers, depth, width = anchor.shape
+    group = lax.axis_size("fsdp")
+    chips = group // 2
     rows = layers * depth // 4
     piece = width // (2 * PIECES)
-    if replicas != 4 or (layers * depth) % (4 * STEP_ROWS) != 0 or width % (256 * PIECES) != 0:
-        spread = anchor - fragment_local[0]
-        return lax.psum(spread, "replica") / replicas
+    out_features = grad.shape[1]
     sems = pltpu.SemaphoreType.DMA
-    mean = pl.pallas_call(
-        functools.partial(outer_kernel, rows, piece),
-        out_shape=jax.ShapeDtypeStruct((4 * rows, width), jnp.float32),
-        in_specs=[pl.BlockSpec(memory_space=pl.ANY)] * 2,
-        out_specs=pl.BlockSpec(memory_space=pl.ANY),
+    return pl.pallas_call(
+        functools.partial(outer_kernel, rows, piece, group),
+        out_shape=(
+            jax.ShapeDtypeStruct((4 * rows, width), jnp.float32),
+            jax.ShapeDtypeStruct((feature_rows, out_features), jnp.float32),
+            jax.ShapeDtypeStruct((8, 128), jnp.float32),
+        ),
+        in_specs=[pl.BlockSpec(memory_space=pl.ANY)] * 3,
+        out_specs=(
+            pl.BlockSpec(memory_space=pl.ANY),
+            pl.BlockSpec(memory_space=pl.ANY),
+            pl.BlockSpec(memory_space=pltpu.VMEM),
+        ),
         scratch_shapes=[
             pltpu.VMEM((4, rows, width), jnp.float32),
             pltpu.VMEM((4, rows, width), jnp.float32),
@@ -207,15 +378,48 @@
             sems((4,)),
             sems((6, 2, PIECES)),
             sems((6, 2, PIECES)),
+            pltpu.VMEM((chips, feature_rows, out_features), jnp.float32),
+            pltpu.VMEM((chips, feature_rows, out_features), jnp.float32),
+            pltpu.VMEM((chips - 1, feature_rows + 16, out_features), jnp.bfloat16),
+            pltpu.VMEM((chips - 1, feature_rows + 16, out_features), jnp.bfloat16),
+            pltpu.VMEM((8, 128), jnp.float32),
+            pltpu.VMEM((group - 1, 8, 128), jnp.float32),
+            sems((chips,)),
+            sems((2, chips)),
+            sems((2, chips - 1)),
+            sems((2, group - 1)),
         ],
         compiler_params=pltpu.CompilerParams(
-            collective_id=0, has_side_effects=True, vmem_limit_bytes=48 * 1024 * 1024
+            collective_id=0, has_side_effects=True, vmem_limit_bytes=50 * 1024 * 1024
         ),
         cost_estimate=pl.CostEstimate(
             flops=40 * layers * depth * width, bytes_accessed=12 * layers * depth * width, transcendentals=0
         ),
-    )(fragment_local.reshape(4 * rows, width), anchor.reshape(4 * rows, width))
-    return mean.reshape(anchor.shape)
+    )(fragment_local.reshape(4 * rows, width), anchor.reshape(4 * rows, width), grad)
+
+
+def outer_step_kernel(mean_ref, anchor_ref, momentum_ref, prev_ref, delta_ref, new_momentum_ref, new_anchor_ref):
+    delta_ref[...] = mean_ref[...]
+    prev = prev_ref[...]
+    momentum = outer_mu * momentum_ref[...] + prev
+    new_momentum_ref[...] = momentum
+    new_anchor_ref[...] = anchor_ref[...] - outer_rate * (prev + outer_mu * momentum)
+
+
+def outer_step(mean, anchor, outer_momentum, outer_prev):
+    rows, width = mean.shape
+    tall = math.gcd(rows, 256)
+    spec = pl.BlockSpec((tall, width), lambda i: (i, 0))
+    flat = jax.ShapeDtypeStruct(mean.shape, jnp.float32)
+    results = pl.pallas_call(
+        outer_step_kernel,
+        grid=(rows // tall,),
+        in_specs=[spec] * 4,
+        out_specs=(spec,) * 3,
+        out_shape=(flat,) * 3,
+        compiler_params=pltpu.CompilerParams(vmem_limit_bytes=32 * 1024 * 1024),
+    )(mean, *(a.reshape(mean.shape) for a in (anchor, outer_momentum, outer_prev)))
+    return tuple(a.reshape(anchor.shape) for a in results)
 
 
 def body(
@@ -232,24 +436,29 @@
     groups = lax.axis_size("fsdp")
     feature_rows = inner_weight.shape[1]
     out_features = inner_weight.shape[2]
-    grad_shard = lax.psum_scatter(
-        lax.dot_general(
-            inputs, out_grad, (((0,), (0,)), ((), ())), preferred_element_type=jnp.float32
-        ),
-        "fsdp",
-        scatter_dimension=0,
-        tiled=True,
+    grad = lax.dot_general(
+        inputs, out_grad, (((0,), (0,)), ((), ())), preferred_element_type=jnp.float32
     )
-    norm_sq = lax.psum(jnp.sum(grad_shard * grad_shard), "fsdp")
+    joint = fits(anchor, grad, feature_rows)
+    if joint:
+        mean, grad_shard, squares = joint_sums(anchor, fragment_local, grad, feature_rows)
+        norm_sq = jnp.sum(squares)
+    else:
+        grad_shard = lax.psum_scatter(grad, "fsdp", scatter_dimension=0, tiled=True)
+        norm_sq = lax.psum(jnp.sum(grad_shard * grad_shard), "fsdp")
     clip_limit = clip_rms * math.sqrt(feature_rows * groups * out_features)
     factor = jnp.minimum(1.0, clip_limit / jnp.sqrt(norm_sq + norm_eps))
     clipped = (grad_shard * factor)[None]
     new_first = first_decay * adam_first + (1.0 - first_decay) * clipped
     new_second = second_decay * adam_second + (1.0 - second_decay) * clipped * clipped
     new_weight = inner_weight - inner_rate * new_first / (jnp.sqrt(new_second) + adam_eps)
-    new_momentum = outer_mu * outer_momentum + outer_prev
-    new_anchor = anchor - outer_rate * (outer_prev + outer_mu * new_momentum)
-    outer_delta = outer_mean(anchor, fragment_local)
+    if joint:
+        outer_delta, new_momentum, new_anchor = outer_step(mean, anchor, outer_momentum, outer_prev)
+    else:
+        new_momentum = outer_mu * outer_momentum + outer_prev
+        new_anchor = anchor - outer_rate * (outer_prev + outer_mu * new_momentum)
+        spread = anchor - fragment_local[0]
+        outer_delta = lax.psum(spread, "replica") / lax.axis_size("replica")
     return (new_weight, new_first, new_second, outer_delta, new_momentum, new_anchor)
 
 

time: 146 us -> 116 us (0.79)
  Pallas kernels: 78.5 us -> 96.3 us
  blocking collectives: 16.8 us -> 0 us
  other arithmetic: 20.1 us -> 3.92 us
  between operations: 14.8 us -> 1.36 us
  local copies, waits for them, and re-layouts: 10.2 us -> 8.36 us
    pallas_call x1 -> x2, Pallas kernels: 78.5 us -> 96.3 us  [the longest x1 80.6 us: joint_sums(): pl.pallas_call(functools.partial(outer_kernel, rows, piece, group), out_s...]
    psum x1 -> x0, blocking collectives: 16.8 us -> none  [body(): norm_sq = lax.psum(jnp.sum(grad_shard * grad_shard), 'fsdp')]
    sub x1 -> x0, other arithmetic: 14.7 us -> none  [body(): new_anchor = anchor - outer_rate * (outer_prev + outer_mu * new_momentum)]
    unnamed x11 -> x12, local copies, waits for them, and re-layouts: 10.2 us -> 8.36 us
    reduce_sum x1, other arithmetic: 2.1 us -> 0.6 us  [body(): norm_sq = jnp.sum(squares)]
  transfers between devices with their start and end apart: 1 -> 0, of which waited for: 0 -> 0; matrix products, arithmetic and copies ran while one was open for 10% -> 0% of each run, Pallas kernels for 54% -> 0%
where the time goes in v2:
time: 116 us
  Pallas kernels  96.3 us (83%)
  local copies, waits for them, and re-layouts  8.36 us (7%)
  matrix products  5.64 us (5%)
  other arithmetic  3.92 us (3%)
  between operations  1.36 us (1%)
    pallas_call x1, Pallas kernels, joint_sums(): pl.pallas_call(functools.partial(outer_kernel, rows, piece, group), out_s...  80.6 us
    pallas_call x1, Pallas kernels, outer_step(): pl.pallas_call(outer_step_kernel, grid=(rows // tall,), in_specs=[spec] *...  15.7 us
    unnamed x12, local copies, waits for them, and re-layouts  8.36 us
    dot_general x1, matrix products, body(): lax.dot_general(inputs, out_grad, (((0,), (0,)), ((), ())), preferred_ele...  5.64 us
    sub x1, other arithmetic, body(): inner_weight - inner_rate * new_first / (jnp.sqrt(new_second) + adam_eps)  3.32 us

profile of v2, /device:TPU:0, one launch (start us, length us, event | category | flops | bytes accessed | tf_op | source)
XLA Modules:
  0.0 115.6 jit_solution(1441479501914945819)
XLA Ops:
  0.6 0.0 copy-start
  0.6 1.6 %copy-done = bf16[256,4096]{1,0:T(8,128)(2,1)S(1)} copy-done((bf16[256,4096]{1,0:T(8,128)(2,1)S(1)}, bf16[256,4096]{1,0:T(8,128)(2,1)}, u32[]{:S(2)}) %copy-start) | copy-done | bytes 2097176
  2.2 5.6 %fusion.3.grad_ref = f32[4096,512]{1,0:T(8,128)} fusion(bf16[256,4096]{1,0:T(8,128)(2,1)S(1)} %copy-done, bf16[256,512]{1,0:T(8,128)(2,1)} %param.10), kind=kOutput, calls=%fused_computation.5 | convolution fusion | flops 1073741824 | bytes 10747904 | tf_op jit(solution)/shard_map/dot_general | solution.py:439
  7.9 0.0 copy-start.4
  7.9 0.0 copy-start.5
  7.9 80.6 %shard_map.136 = (f32[2048,1024]{1,0:T(8,128)}, f32[512,512]{1,0:T(8,128)S(1)}, f32[8,128]{1,0:T(8,128)S(1)}) custom-call(f32[2048,1024]{1,0:T(8,128)} %bitcast.19, f32[2048,1024]{1,0:T(8,128)} %bitcast.17, f32[4096,512]{1,0:T(8,128)} %fusion.3.grad_ref), custom_call_target="tpu_custom_call" | custom-call | flops 83886080 | bytes 25165824 | tf_op jit(solution)/shard_map/pallas_call | solution.py:359
  88.4 0.6 reduce_sum.9
  89.7 0.0 copy-done.4
  89.7 0.0 copy-done.5
  89.7 3.3 %divide_subtract_fusion = (f32[1,512,512]{2,1,0:T(8,128)}, f32[1,512,512]{2,1,0:T(8,128)}, f32[1,512,512]{2,1,0:T(8,128)}) fusion(f32[1,512,512]{2,1,0:T(8,128)S(1)} %copy-done.4, f32[512,512]{1,0:T(8,128)S(1)} %get-tuple-element.12, f32[]{:T(128)S(6)} %min_shard_map.3, f32[1,512,512]{2,1,0:T(8,128)S(1)} %copy-done.5, f32[1,512,512]{2,1,0:T(8,128)} %param.13), kind=kLoop, calls=%fused_computation.4 | loop fusion | flops 3145728 | bytes 7340036 | tf_op jit(solution)/shard_map/sub | solution.py:454
  93.1 0.0 copy-start.2
  93.1 3.4 %copy-done.2 = f32[2,1024,1024]{2,1,0:T(8,128)S(1)} copy-done((f32[2,1024,1024]{2,1,0:T(8,128)S(1)}, f32[2,1024,1024]{2,1,0:T(8,128)}, u32[]{:S(2)}) %copy-start.2) | copy-done | bytes 8388632
  96.4 0.0 copy-start.3
  96.5 3.4 %copy-done.3 = f32[2048,1024]{1,0:T(8,128)S(1)} copy-done((f32[2048,1024]{1,0:T(8,128)S(1)}, f32[2048,1024]{1,0:T(8,128)}, u32[]{:S(2)}) %copy-start.3) | copy-done | bytes 8388632
  99.8 0.0 copy-start.1
  99.8 15.7 %shard_map.137 = (f32[2048,1024]{1,0:T(8,128)}, f32[2048,1024]{1,0:T(8,128)}, f32[2048,1024]{1,0:T(8,128)}) custom-call(f32[2048,1024]{1,0:T(8,128)S(1)} %copy-done.3, f32[2048,1024]{1,0:T(8,128)S(1)} %bitcast.18, f32[2048,1024]{1,0:T(8,128)} %bitcast.20, f32[2048,1024]{1,0:T(8,128)} %bitcast.21), custom_call_target="tpu_custom_call" | custom-call | tf_op jit(solution)/shard_map/pallas_call | solution.py:414
  115.5 0.0 copy-done.1
Async XLA Ops:
  0.6 1.6 %copy-start = (bf16[256,4096]{1,0:T(8,128)(2,1)S(1)}, bf16[256,4096]{1,0:T(8,128)(2,1)}, u32[]{:S(2)}) copy-start(bf16[256,4096]{1,0:T(8,128)(2,1)} %param.9) | copy-start | bytes 6291460
  7.9 81.9 %copy-start.4 = (f32[1,512,512]{2,1,0:T(8,128)S(1)}, f32[1,512,512]{2,1,0:T(8,128)}, u32[]{:S(2)}) copy-start(f32[1,512,512]{2,1,0:T(8,128)} %param.11) | copy-start | bytes 3145732
  7.9 81.9 %copy-start.5 = (f32[1,512,512]{2,1,0:T(8,128)S(1)}, f32[1,512,512]{2,1,0:T(8,128)}, u32[]{:S(2)}) copy-start(f32[1,512,512]{2,1,0:T(8,128)} %param.12) | copy-start | bytes 3145732
  93.1 3.4 %copy-start.2 = (f32[2,1024,1024]{2,1,0:T(8,128)S(1)}, f32[2,1024,1024]{2,1,0:T(8,128)}, u32[]{:S(2)}) copy-start(f32[2,1024,1024]{2,1,0:T(8,128)} %param.15) | copy-start | bytes 25165828
  96.4 3.4 %copy-start.3 = (f32[2048,1024]{1,0:T(8,128)S(1)}, f32[2048,1024]{1,0:T(8,128)}, u32[]{:S(2)}) copy-start(f32[2048,1024]{1,0:T(8,128)} %get-tuple-element.14.mean_ref) | copy-start | bytes 25165828
  99.8 15.7 %copy-start.1 = (bf16[256,4096]{1,0:T(8,128)(2,1)S(1)}, bf16[256,4096]{1,0:T(8,128)(2,1)}, u32[]{:S(2)}) copy-start(bf16[256,4096]{1,0:T(8,128)(2,1)} %param.9) | copy-start | bytes 6291460

commit v3 on v2

--- a/solution.py
+++ b/solution.py
@@ -31,7 +31,8 @@
     group,
     local_ref,
     anchor_ref,
-    grad_ref,
+    inputs_ref,
+    out_grad_ref,
     out_ref,
     shard_ref,
     norm_ref,
@@ -44,12 +45,13 @@
     send_sem,
     recv_sem,
     own,
+    other,
     twin,
     grad_sent,
     grad_held,
     part_sent,
     part_held,
-    own_sem,
+    shard_sem,
     twin_sem,
     grad_sem,
     part_sem,
@@ -69,14 +71,18 @@
     block = shard_ref.shape[0]
     grad_steps = block // STEP_ROWS
 
-    def own_copy(s):
-        start = pl.multiple_of((((chip + s) % chips) * 2 + core) * block, block)
-        return pltpu.make_async_copy(grad_ref.at[pl.ds(start, block), :], own.at[s], own_sem.at[s])
+    def term(s, owner_core):
+        start = pl.multiple_of((((chip + s) % chips) * 2 + owner_core) * block, block)
+        return lax.dot_general(
+            inputs_ref[:, pl.ds(start, block)],
+            out_grad_ref[...],
+            (((0,), (0,)), ((), ())),
+            preferred_element_type=jnp.float32,
+        )
 
     def twin_copy(s):
-        start = pl.multiple_of((((chip + s) % chips) * 2 + 1 - core) * block, block)
         return pltpu.make_async_remote_copy(
-            src_ref=grad_ref.at[pl.ds(start, block), :],
+            src_ref=other.at[s],
             dst_ref=twin.at[s],
             send_sem=twin_sem.at[0, s],
             recv_sem=twin_sem.at[1, s],
@@ -125,10 +131,6 @@
             barrier, inc=1, device_id={"fsdp": (place + s) % group}, device_id_type=pl.DeviceIdType.MESH
         )
     pl.semaphore_wait(barrier, group + 1)
-
-    for s in range(chips):
-        own_copy(s).start()
-        twin_copy(s).start()
 
     def columns(half, k):
         return pl.ds((half * PIECES + k) * width, width)
@@ -253,14 +255,19 @@
         for way in (0, 1):
             encode(0, 1 - way, k, KIND_A, way, ())
             copy(KIND_A, way, k).start()
+    farthest_first = (2, 1, 3, 0) if chips == 4 else (*range(1, chips), 0)
+    for s in farthest_first:
+        other[s, :, :] = term(s, 1 - core)
+        twin_copy(s).start()
     loaded(1)
     loaded(2)
     for k in range(PIECES):
         for way in (0, 1):
             encode(1 + way, 1 - way, k, KIND_B, way, ())
             copy(KIND_B, way, k).start()
-    for s in (2, 1, 3) if chips == 4 else range(1, chips):
-        own_copy(s).wait()
+    for s in farthest_first:
+        own[s, :, :] = term(s, core)
+    for s in farthest_first[:-1]:
         twin_copy(s).wait_recv()
         encode_grad(s)
         grad_copy(s).start()
@@ -278,14 +285,13 @@
             for way in (0, 1):
                 copy(KIND_G0 + half, way, k).start()
 
-    own_copy(0).wait()
     twin_copy(0).wait_recv()
     for s in range(1, chips):
         grad_copy(s).wait_recv()
     reduce_grad()
     for s in range(1, group):
         part_copy(s).start()
-    shard_store = pltpu.make_async_copy(own.at[0], shard_ref, own_sem.at[0])
+    shard_store = pltpu.make_async_copy(own.at[0], shard_ref, shard_sem)
     shard_store.start()
 
     def store(j):
@@ -335,7 +341,7 @@
         store(j).wait()
 
 
-def fits(anchor, grad, feature_rows):
+def fits(anchor, out_grad, feature_rows):
     layers, depth, width = anchor.shape
     return (
         lax.axis_size("replica") == 4
@@ -343,18 +349,18 @@
         and width % (256 * PIECES) == 0
         and lax.axis_size("fsdp") == 8
         and feature_rows % STEP_ROWS == 0
-        and grad.shape[1] % 128 == 0
+        and out_grad.shape[1] % 128 == 0
         and layers * depth * width <= 2 * 1024 * 1024
     )
 
 
-def joint_sums(anchor, fragment_local, grad, feature_rows):
+def joint_sums(anchor, fragment_local, inputs, out_grad, feature_rows):
     layers, depth, width = anchor.shape
     group = lax.axis_size("fsdp")
     chips = group // 2
     rows = layers * depth // 4
     piece = width // (2 * PIECES)
-    out_features = grad.shape[1]
+    out_features = out_grad.shape[1]
     sems = pltpu.SemaphoreType.DMA
     return pl.pallas_call(
         functools.partial(outer_kernel, rows, piece, group),
@@ -363,7 +369,7 @@
             jax.ShapeDtypeStruct((feature_rows, out_features), jnp.float32),
             jax.ShapeDtypeStruct((8, 128), jnp.float32),
         ),
-        in_specs=[pl.BlockSpec(memory_space=pl.ANY)] * 3,
+        in_specs=[pl.BlockSpec(memory_space=pl.ANY)] * 2 + [pl.BlockSpec(memory_space=pltpu.VMEM)] * 2,
         out_specs=(
             pl.BlockSpec(memory_space=pl.ANY),
             pl.BlockSpec(memory_space=pl.ANY),
@@ -380,22 +386,23 @@
             sems((6, 2, PIECES)),
             pltpu.VMEM((chips, feature_rows, out_features), jnp.float32),
             pltpu.VMEM((chips, feature_rows, out_features), jnp.float32),
+            pltpu.VMEM((chips, feature_rows, out_features), jnp.float32),
             pltpu.VMEM((chips - 1, feature_rows + 16, out_features), jnp.bfloat16),
             pltpu.VMEM((chips - 1, feature_rows + 16, out_features), jnp.bfloat16),
             pltpu.VMEM((8, 128), jnp.float32),
             pltpu.VMEM((group - 1, 8, 128), jnp.float32),
-            sems((chips,)),
+            sems,
             sems((2, chips)),
             sems((2, chips - 1)),
             sems((2, group - 1)),
         ],
         compiler_params=pltpu.CompilerParams(
-            collective_id=0, has_side_effects=True, vmem_limit_bytes=50 * 1024 * 1024
+            collective_id=0, has_side_effects=True, vmem_limit_bytes=46 * 1024 * 1024
         ),
         cost_estimate=pl.CostEstimate(
             flops=40 * layers * depth * width, bytes_accessed=12 * layers * depth * width, transcendentals=0
         ),
-    )(fragment_local.reshape(4 * rows, width), anchor.reshape(4 * rows, width), grad)
+    )(fragment_local.reshape(4 * rows, width), anchor.reshape(4 * rows, width), inputs, out_grad)
 
 
 def outer_step_kernel(mean_ref, anchor_ref, momentum_ref, prev_ref, delta_ref, new_momentum_ref, new_anchor_ref):
@@ -417,7 +424,7 @@
         in_specs=[spec] * 4,
         out_specs=(spec,) * 3,
         out_shape=(flat,) * 3,
-        compiler_params=pltpu.CompilerParams(vmem_limit_bytes=32 * 1024 * 1024),
+        compiler_params=pltpu.CompilerParams(vmem_limit_bytes=58 * 1024 * 1024),
     )(mean, *(a.reshape(mean.shape) for a in (anchor, outer_momentum, outer_prev)))
     return tuple(a.reshape(anchor.shape) for a in results)
 
@@ -436,14 +443,14 @@
     groups = lax.axis_size("fsdp")
     feature_rows = inner_weight.shape[1]
     out_features = inner_weight.shape[2]
-    grad = lax.dot_general(
-        inputs, out_grad, (((0,), (0,)), ((), ())), preferred_element_type=jnp.float32
-    )
-    joint = fits(anchor, grad, feature_rows)
+    joint = fits(anchor, out_grad, feature_rows)
     if joint:
-        mean, grad_shard, squares = joint_sums(anchor, fragment_local, grad, feature_rows)
+        mean, grad_shard, squares = joint_sums(anchor, fragment_local, inputs, out_grad, feature_rows)
         norm_sq = jnp.sum(squares)
     else:
+        grad = lax.dot_general(
+            inputs, out_grad, (((0,), (0,)), ((), ())), preferred_element_type=jnp.float32
+        )
         grad_shard = lax.psum_scatter(grad, "fsdp", scatter_dimension=0, tiled=True)
         norm_sq = lax.psum(jnp.sum(grad_shard * grad_shard), "fsdp")
     clip_limit = clip_rms * math.sqrt(feature_rows * groups * out_features)

time: 116 us -> 109 us (0.940)
  local copies, waits for them, and re-layouts: 8.36 us -> 2.54 us
  matrix products: 5.64 us -> 0 us
  Pallas kernels: 96.3 us -> 101 us
    unnamed x12 -> x8, local copies, waits for them, and re-layouts: 8.36 us -> 2.54 us
    dot_general x1 -> x0, matrix products: 5.64 us -> none  [body(): lax.dot_general(inputs, out_grad, (((0,), (0,)), ((), ())), preferred_ele...]
    pallas_call x1, Pallas kernels: 15.7 us -> 20.1 us  [outer_step(): pl.pallas_call(outer_step_kernel, grid=(rows // tall,), in_specs=[spec] *...]
where the time goes in v3:
time: 109 us; the launch traced here: 108 us
  Pallas kernels  101 us (93%)
  other arithmetic  3.92 us (4%)
  local copies, waits for them, and re-layouts  2.54 us (2%)
  between operations  1.36 us (1%)
    pallas_call x1, Pallas kernels, joint_sums(): pl.pallas_call(functools.partial(outer_kernel, rows, piece, group), out_s...  80.5 us
    pallas_call x1, Pallas kernels, outer_step(): pl.pallas_call(outer_step_kernel, grid=(rows // tall,), in_specs=[spec] *...  20.1 us
    sub x1, other arithmetic, body(): inner_weight - inner_rate * new_first / (jnp.sqrt(new_second) + adam_eps)  3.32 us
    unnamed x8, local copies, waits for them, and re-layouts  2.54 us

profile of v3, /device:TPU:0, one launch (start us, length us, event | category | flops | bytes accessed | tf_op | source)
XLA Modules:
  0.0 108.4 jit_solution(17648154269689674329)
XLA Ops:
  0.6 0.0 copy-start
  0.6 1.6 %copy-done = bf16[256,4096]{1,0:T(8,128)(2,1)S(1)} copy-done((bf16[256,4096]{1,0:T(8,128)(2,1)S(1)}, bf16[256,4096]{1,0:T(8,128)(2,1)}, u32[]{:S(2)}) %copy-start) | copy-done | bytes 2097176
  2.2 0.0 copy-start.1
  2.2 0.9 copy-done.1
  3.2 0.0 copy-start.2
  3.2 0.0 copy-start.3
  3.2 80.5 %shard_map.136 = (f32[2048,1024]{1,0:T(8,128)}, f32[512,512]{1,0:T(8,128)S(1)}, f32[8,128]{1,0:T(8,128)S(1)}) custom-call(f32[2048,1024]{1,0:T(8,128)} %bitcast.17, f32[2048,1024]{1,0:T(8,128)} %bitcast.15, bf16[256,4096]{1,0:T(8,128)(2,1)S(1)} %copy-done, bf16[256,512]{1,0:T(8,128)(2,1)S(1)} %copy-done.1), custom_call_target="tpu_custom_call" | custom-call | flops 83886080 | bytes 25165824 | tf_op jit(solution)/shard_map/pallas_call | solution.py:365
  83.7 0.6 reduce_sum.9
  85.0 0.0 copy-done.2
  85.0 0.0 copy-done.3
  85.0 3.3 %divide_subtract_fusion = (f32[1,512,512]{2,1,0:T(8,128)}, f32[1,512,512]{2,1,0:T(8,128)}, f32[1,512,512]{2,1,0:T(8,128)}) fusion(f32[1,512,512]{2,1,0:T(8,128)S(1)} %copy-done.2, f32[512,512]{1,0:T(8,128)S(1)} %get-tuple-element.12, f32[]{:T(128)S(6)} %min_shard_map.3, f32[1,512,512]{2,1,0:T(8,128)S(1)} %copy-done.3, f32[1,512,512]{2,1,0:T(8,128)} %param.13), kind=kLoop, calls=%fused_computation.4 | loop fusion | flops 3145728 | bytes 7340036 | tf_op jit(solution)/shard_map/sub | solution.py:461
  88.3 20.1 %shard_map.137 = (f32[2048,1024]{1,0:T(8,128)}, f32[2048,1024]{1,0:T(8,128)}, f32[2048,1024]{1,0:T(8,128)}) custom-call(f32[2048,1024]{1,0:T(8,128)} %get-tuple-element.14.mean_ref, f32[2048,1024]{1,0:T(8,128)} %bitcast.16, f32[2048,1024]{1,0:T(8,128)} %bitcast.18, f32[2048,1024]{1,0:T(8,128)} %bitcast.19), custom_call_target="tpu_custom_call" | custom-call | tf_op jit(solution)/shard_map/pallas_call | solution.py:421
Async XLA Ops:
  0.6 1.6 %copy-start = (bf16[256,4096]{1,0:T(8,128)(2,1)S(1)}, bf16[256,4096]{1,0:T(8,128)(2,1)}, u32[]{:S(2)}) copy-start(bf16[256,4096]{1,0:T(8,128)(2,1)} %inputs_ref.1) | copy-start | bytes 6291460
  2.2 0.9 copy-start.1
  3.2 81.8 %copy-start.2 = (f32[1,512,512]{2,1,0:T(8,128)S(1)}, f32[1,512,512]{2,1,0:T(8,128)}, u32[]{:S(2)}) copy-start(f32[1,512,512]{2,1,0:T(8,128)} %param.11) | copy-start | bytes 3145732
  3.2 81.8 %copy-start.3 = (f32[1,512,512]{2,1,0:T(8,128)S(1)}, f32[1,512,512]{2,1,0:T(8,128)}, u32[]{:S(2)}) copy-start(f32[1,512,512]{2,1,0:T(8,128)} %param.12) | copy-start | bytes 3145732

commit v4 on v3

--- a/solution.py
+++ b/solution.py
@@ -36,12 +36,10 @@
     out_ref,
     shard_ref,
     norm_ref,
-    vf,
     va,
     sent,
     held,
     load_sem,
-    store_sem,
     send_sem,
     recv_sem,
     own,
@@ -115,7 +113,7 @@
         part = pl.ds(pl.multiple_of(owners[j] * rows, rows), rows)
         loads.append(
             (
-                pltpu.make_async_copy(local_ref.at[part, :], vf.at[j], load_sem.at[j, 0]),
+                pltpu.make_async_copy(local_ref.at[part, :], out_ref.at[part, :], load_sem.at[j, 0]),
                 pltpu.make_async_copy(anchor_ref.at[part, :], va.at[j], load_sem.at[j, 1]),
             )
         )
@@ -131,6 +129,9 @@
             barrier, inc=1, device_id={"fsdp": (place + s) % group}, device_id_type=pl.DeviceIdType.MESH
         )
     pl.semaphore_wait(barrier, group + 1)
+
+    def spot(j, i):
+        return pl.ds(pl.multiple_of(owners[j] * rows + i * STEP_ROWS, STEP_ROWS), STEP_ROWS)
 
     def columns(half, k):
         return pl.ds((half * PIECES + k) * width, width)
@@ -165,12 +166,12 @@
 
         def gather(i, top):
             r = pl.ds(pl.multiple_of(i * STEP_ROWS, STEP_ROWS), STEP_ROWS)
-            x = va[j, r, cs] - vf[j, r, cs]
+            x = va[j, r, cs] - out_ref[spot(j, i), cs]
             for t, s in zip(terms, scales):
                 x = x + decoded(held, t[0], t[1], k, s, r)
             if factor is not None:
                 x = x * factor
-            vf[j, r, cs] = x
+            out_ref[spot(j, i), cs] = x
             return jnp.maximum(top, jnp.max(jnp.abs(x).reshape(STEP_ROWS // 8, 8, width), axis=0))
 
         top = lax.fori_loop(0, steps, gather, jnp.zeros((8, width), jnp.float32))
@@ -182,7 +183,7 @@
 
         def write(i, c):
             r = pl.ds(pl.multiple_of(i * STEP_ROWS, STEP_ROWS), STEP_ROWS)
-            x = vf[j, r, cs]
+            x = out_ref[spot(j, i), cs]
             y = jnp.exp(jnp.abs(x) * slope - HALF_SPAN)
             sent[kind, way, k, r, :] = jnp.where(x < 0.0, -y, y).astype(jnp.bfloat16)
             return c
@@ -195,7 +196,7 @@
 
         def step(i, c):
             r = pl.ds(pl.multiple_of(i * STEP_ROWS, STEP_ROWS), STEP_ROWS)
-            vf[j, r, cs] = decoded(box, kind, way, k, scale, r)
+            out_ref[spot(j, i), cs] = decoded(box, kind, way, k, scale, r)
             return c
 
         lax.fori_loop(0, steps, step, 0)
@@ -294,14 +295,9 @@
     shard_store = pltpu.make_async_copy(own.at[0], shard_ref, shard_sem)
     shard_store.start()
 
-    def store(j):
-        part = pl.ds(pl.multiple_of(owners[j] * rows, rows), rows)
-        return pltpu.make_async_copy(vf.at[j], out_ref.at[part, :], store_sem.at[j])
-
     for k in range(PIECES):
         for half in (0, 1):
             unfold(3, half, k, sent, KIND_G0 + half, 0)
-    store(3).start()
     for k in range(PIECES):
         for way in (0, 1):
             first = KIND_G1 if way == 0 else KIND_G0
@@ -315,12 +311,10 @@
             late = 1 - way
             copy(KIND_G0 + late, way, k).wait_recv()
             unfold(1 + way, late, k, held, KIND_G0 + late, way)
-        store(1 + way).start()
     for k in range(PIECES):
         for way in (0, 1):
             copy(KIND_F, way, k).wait_recv()
             unfold(0, 1 - way, k, held, KIND_F, way)
-    store(0).start()
     norm = part_sent[...]
     for s in range(1, group):
         part_copy(s).wait_recv()
@@ -337,8 +331,6 @@
         for way in (0, 1):
             for k in range(PIECES):
                 copy(kind, way, k).wait_send()
-    for j in range(4):
-        store(j).wait()
 
 
 def fits(anchor, out_grad, feature_rows):
@@ -371,17 +363,15 @@
         ),
         in_specs=[pl.BlockSpec(memory_space=pl.ANY)] * 2 + [pl.BlockSpec(memory_space=pltpu.VMEM)] * 2,
         out_specs=(
-            pl.BlockSpec(memory_space=pl.ANY),
+            pl.BlockSpec(memory_space=pltpu.VMEM),
             pl.BlockSpec(memory_space=pl.ANY),
             pl.BlockSpec(memory_space=pltpu.VMEM),
         ),
         scratch_shapes=[
             pltpu.VMEM((4, rows, width), jnp.float32),
-            pltpu.VMEM((4, rows, width), jnp.float32),
             pltpu.VMEM((5, 2, PIECES, rows + 16, piece), jnp.bfloat16),
             pltpu.VMEM((6, 2, PIECES, rows + 16, piece), jnp.bfloat16),
             sems((4, 2)),
-            sems((4,)),
             sems((6, 2, PIECES)),
             sems((6, 2, PIECES)),
             pltpu.VMEM((chips, feature_rows, out_features), jnp.float32),
@@ -397,7 +387,7 @@
             sems((2, group - 1)),
         ],
         compiler_params=pltpu.CompilerParams(
-            collective_id=0, has_side_effects=True, vmem_limit_bytes=46 * 1024 * 1024
+            collective_id=0, has_side_effects=True, vmem_limit_bytes=38 * 1024 * 1024
         ),
         cost_estimate=pl.CostEstimate(
             flops=40 * layers * depth * width, bytes_accessed=12 * layers * depth * width, transcendentals=0
@@ -415,7 +405,7 @@
 
 def outer_step(mean, anchor, outer_momentum, outer_prev):
     rows, width = mean.shape
-    tall = math.gcd(rows, 256)
+    tall = math.gcd(rows, 128)
     spec = pl.BlockSpec((tall, width), lambda i: (i, 0))
     flat = jax.ShapeDtypeStruct(mean.shape, jnp.float32)
     results = pl.pallas_call(
@@ -424,7 +414,7 @@
         in_specs=[spec] * 4,
         out_specs=(spec,) * 3,
         out_shape=(flat,) * 3,
-        compiler_params=pltpu.CompilerParams(vmem_limit_bytes=58 * 1024 * 1024),
+        compiler_params=pltpu.CompilerParams(vmem_limit_bytes=44 * 1024 * 1024),
     )(mean, *(a.reshape(mean.shape) for a in (anchor, outer_momentum, outer_prev)))
     return tuple(a.reshape(anchor.shape) for a in results)
 
@@ -446,6 +436,8 @@
     joint = fits(anchor, out_grad, feature_rows)
     if joint:
         mean, grad_shard, squares = joint_sums(anchor, fragment_local, inputs, out_grad, feature_rows)
+        outer_delta, new_momentum, new_anchor = outer_step(mean, anchor, outer_momentum, outer_prev)
+        squares, outer_delta = lax.optimization_barrier((squares, outer_delta))
         norm_sq = jnp.sum(squares)
     else:
         grad = lax.dot_general(
@@ -459,9 +451,7 @@
     new_first = first_decay * adam_first + (1.0 - first_decay) * clipped
     new_second = second_decay * adam_second + (1.0 - second_decay) * clipped * clipped
     new_weight = inner_weight - inner_rate * new_first / (jnp.sqrt(new_second) + adam_eps)
-    if joint:
-        outer_delta, new_momentum, new_anchor = outer_step(mean, anchor, outer_momentum, outer_prev)
-    else:
+    if not joint:
         new_momentum = outer_mu * outer_momentum + outer_prev
         new_anchor = anchor - outer_rate * (outer_prev + outer_mu * new_momentum)
         spread = anchor - fragment_local[0]

time: 109 us -> 110 us (level)
    pallas_call x1, Pallas kernels: 20.1 us -> 22.6 us  [outer_step(): pl.pallas_call(outer_step_kernel, grid=(rows // tall,), in_specs=[spec] *...]
    pallas_call x1, Pallas kernels: 80.5 us -> 79.2 us  [joint_sums(): pl.pallas_call(functools.partial(outer_kernel, rows, piece, group), out_s...]
where the time goes in v4:
time: 110 us
  Pallas kernels  102 us (93%)
  other arithmetic  3.88 us (4%)
  local copies, waits for them, and re-layouts  2.55 us (2%)
  between operations  1.37 us (1%)
    pallas_call x1, Pallas kernels, joint_sums(): pl.pallas_call(functools.partial(outer_kernel, rows, piece, group), out_s...  79.2 us
    pallas_call x1, Pallas kernels, outer_step(): pl.pallas_call(outer_step_kernel, grid=(rows // tall,), in_specs=[spec] *...  22.6 us
    sub x1, other arithmetic, body(): inner_weight - inner_rate * new_first / (jnp.sqrt(new_second) + adam_eps)  3.28 us
    unnamed x8, local copies, waits for them, and re-layouts  2.55 us

profile of v4, /device:TPU:0, one launch (start us, length us, event | category | flops | bytes accessed | tf_op | source)
XLA Modules:
  0.0 109.6 jit_solution(11646805112767829002)
XLA Ops:
  0.6 0.0 copy-start
  0.6 1.6 %copy-done = bf16[256,4096]{1,0:T(8,128)(2,1)S(1)} copy-done((bf16[256,4096]{1,0:T(8,128)(2,1)S(1)}, bf16[256,4096]{1,0:T(8,128)(2,1)}, u32[]{:S(2)}) %copy-start) | copy-done | bytes 2097176
  2.2 0.0 copy-start.1
  2.2 0.9 copy-done.1
  3.2 79.2 %shard_map.136 = (f32[2048,1024]{1,0:T(8,128)S(1)}, f32[512,512]{1,0:T(8,128)S(1)}, f32[8,128]{1,0:T(8,128)S(1)}) custom-call(f32[2048,1024]{1,0:T(8,128)} %bitcast.17, f32[2048,1024]{1,0:T(8,128)} %bitcast.15, bf16[256,4096]{1,0:T(8,128)(2,1)S(1)} %copy-done, bf16[256,512]{1,0:T(8,128)(2,1)S(1)} %copy-done.1), custom_call_target="tpu_custom_call" | custom-call | flops 83886080 | bytes 25165824 | tf_op jit(solution)/shard_map/pallas_call | solution.py:357
  82.4 0.0 copy-start.2
  82.4 0.0 copy-start.3
  82.4 22.6 %shard_map.137 = (f32[2048,1024]{1,0:T(8,128)}, f32[2048,1024]{1,0:T(8,128)}, f32[2048,1024]{1,0:T(8,128)}) custom-call(f32[2048,1024]{1,0:T(8,128)S(1)} %get-tuple-element.16.mean_ref, f32[2048,1024]{1,0:T(8,128)} %bitcast.16, f32[2048,1024]{1,0:T(8,128)} %bitcast.18, f32[2048,1024]{1,0:T(8,128)} %bitcast.19), custom_call_target="tpu_custom_call" | custom-call | tf_op jit(solution)/shard_map/pallas_call | solution.py:411
  105.0 0.6 reduce_sum.9
  106.3 0.0 copy-done.2
  106.3 0.0 copy-done.3
  106.3 3.3 %divide_subtract_fusion = (f32[1,512,512]{2,1,0:T(8,128)}, f32[1,512,512]{2,1,0:T(8,128)}, f32[1,512,512]{2,1,0:T(8,128)}) fusion(f32[1,512,512]{2,1,0:T(8,128)S(1)} %copy-done.2, f32[512,512]{1,0:T(8,128)S(1)} %get-tuple-element.14, f32[]{:T(128)S(6)} %min_shard_map.3, f32[1,512,512]{2,1,0:T(8,128)S(1)} %copy-done.3, f32[1,512,512]{2,1,0:T(8,128)} %param.13), kind=kLoop, calls=%fused_computation.4 | loop fusion | flops 3145728 | bytes 7340036 | tf_op jit(solution)/shard_map/sub | solution.py:453
Async XLA Ops:
  0.6 1.6 %copy-start = (bf16[256,4096]{1,0:T(8,128)(2,1)S(1)}, bf16[256,4096]{1,0:T(8,128)(2,1)}, u32[]{:S(2)}) copy-start(bf16[256,4096]{1,0:T(8,128)(2,1)} %inputs_ref.1) | copy-start | bytes 6291460
  2.2 0.9 copy-start.1
  82.4 23.9 %copy-start.2 = (f32[1,512,512]{2,1,0:T(8,128)S(1)}, f32[1,512,512]{2,1,0:T(8,128)}, u32[]{:S(2)}) copy-start(f32[1,512,512]{2,1,0:T(8,128)} %param.11) | copy-start | bytes 3145732
  82.4 23.9 %copy-start.3 = (f32[1,512,512]{2,1,0:T(8,128)S(1)}, f32[1,512,512]{2,1,0:T(8,128)}, u32[]{:S(2)}) copy-start(f32[1,512,512]{2,1,0:T(8,128)} %param.12) | copy-start | bytes 3145732
